TPU v7x, 256 devices: a whole 4x4x8 slice. The times are simulated.
256 devices in a mesh: row: 16 (over x, z_lo), col: 16 (over y, z_hi, core).
Axes of the slice: x: 4, y: 4, z: 8 (z_hi: 2, z_lo: 4; z = z_hi * 4 + z_lo), core: 2. Of those that a mesh axis runs over, the one named last changes fastest.
Arguments:
- tokens: bfloat16 [512, 16384], P('col', 'row'), may hold values from -6 to 6
- gate_codes: bfloat16 [16384, 28672], P('row', 'col'), may hold values from -0.046875 to 0.046875
- gate_scale: float32 [64, 112], P('row', 'col'), may hold values from 0.5 to 5
- up_codes: bfloat16 [16384, 28672], P('row', 'col'), may hold values from -0.046875 to 0.046875
- up_scale: float32 [64, 112], P('row', 'col'), may hold values from 0.5 to 5
- gate_keep: int32 [64, 112], P('row', 'col'), may hold values from 0 to 1, as said below
- down_codes: bfloat16 [28672, 16384], P('col', 'row'), may hold values from -0.03125 to 0.03125
- down_scale: float32 [112, 64], P('col', 'row'), may hold values from 0.5 to 5
- down_keep: int32 [112, 64], P('col', 'row'), may hold values from 0 to 1, as said below
Outputs:
- mixed: bfloat16 [512, 16384], P('col', 'row')
Inputs may be any that keep to these rules, and one draw needn't show every extreme that they name: `gate_keep`: 1 keeps a tile and 0 drops it. One device's block of tiles keeps at most 19, and some block keeps exactly that many in every draw; two blocks at the same col index whose row indices differ by half the row axis keep exactly 22 tiles together. `down_keep`: 1 keeps a tile and 0 drops it.
All inputs are finite; a program needn't handle non-finite values.
Results may differ from a plain program's by a relative error of at most 0.0071.
Values may be sent and summed in bfloat16 or wider, within the bound.
A program may use at most 128 MiB of HBM per device.

v0:
```python
import jax
import jax.numpy as jnp
from jax import lax
from jax.sharding import PartitionSpec as P


def dequantize(codes, scale, keep):
    tile_rows, tile_cols = scale.shape
    rows, cols = codes.shape
    factor = scale * keep.astype(jnp.float32)
    values = codes.astype(jnp.float32).reshape(
        tile_rows, rows // tile_rows, tile_cols, cols // tile_cols
    )
    values = values * factor[:, None, :, None]
    return values.reshape(rows, cols).astype(jnp.bfloat16)


def swiglu(sums, width):
    return (jax.nn.silu(sums[:, :width]) * sums[:, width:]).astype(jnp.bfloat16)


def per_device(
    tokens, gate_codes, gate_scale, up_codes, up_scale, gate_keep, down_codes, down_scale, down_keep
):
    width = gate_codes.shape[1]
    panel = lax.all_gather(tokens, "col", axis=0, tiled=True)
    weight_both = jnp.concatenate(
        [dequantize(gate_codes, gate_scale, gate_keep), dequantize(up_codes, up_scale, gate_keep)],
        axis=1,
    )
    rows = panel
    sums = lax.psum_scatter(
        jnp.dot(rows, weight_both, preferred_element_type=jnp.float32),
        "row",
        scatter_dimension=0,
        tiled=True,
    )
    hidden = swiglu(sums, width)
    hidden_all = lax.all_gather(hidden, "row", axis=0, tiled=True)
    weight_down = dequantize(down_codes, down_scale, down_keep)
    rows = hidden_all
    mixed = lax.psum_scatter(
        jnp.dot(rows, weight_down, preferred_element_type=jnp.float32),
        "col",
        scatter_dimension=0,
        tiled=True,
    )
    return mixed.astype(jnp.bfloat16)


def solution(mesh):
    placed = (
        P("col", "row"),
        P("row", "col"),
        P("row", "col"),
        P("row", "col"),
        P("row", "col"),
        P("row", "col"),
        P("col", "row"),
        P("col", "row"),
        P("col", "row"),
    )
    return jax.shard_map(
        per_device, mesh=mesh, in_specs=placed, out_specs=P("col", "row"), check_vma=False
    )
```

profile of v0, /device:TPU:1, one launch (start us, length us, event | category | flops | bytes accessed | tf_op | source)
XLA Modules:
  0.0 436.1 jit_solution(8626635405215239277)
XLA Ops:
  6.5 0.0 all-gather.3.cloned.1.call-start
  6.5 0.7 all-gather.3.cloned.1.call-update
  7.3 0.0 reduce-scatter.7.cloned.1.call-start
  7.3 0.7 convert_multiply_fusion.2
  8.0 0.1 copy.25
  8.1 1.0 mul.54
  9.1 4.7 %copy.32 = f32[224,8,4,256]{3,1,2,0:T(8,128)} copy(f32[224,8,4,256]{3,2,1,0:T(4,128)S(1)} %bitcast.21) | data formatting | bytes 14680064
  13.9 0.1 copy.23
  14.0 1.0 mul.50
  15.0 4.8 %copy.31 = f32[224,8,4,256]{3,1,2,0:T(8,128)} copy(f32[224,8,4,256]{3,2,1,0:T(4,128)S(1)} %bitcast.22) | data formatting | bytes 14680064
  19.8 6.0 %copy.22 = bf16[1024,1792]{0,1:T(8,128)(2,1)} copy(bf16[1024,1792]{1,0:T(8,128)(2,1)} %param.10) | data formatting | bytes 7340032 | tf_op args[1]
  25.8 5.9 %copy.24 = bf16[1024,1792]{0,1:T(8,128)(2,1)} copy(bf16[1024,1792]{1,0:T(8,128)(2,1)} %param.12) | data formatting | bytes 7340032 | tf_op args[3]
  31.7 11.8 %multiply_convert_fusion.1 = (bf16[1024,1792]{0,1:T(8,128)(2,1)}, bf16[1024,1792]{0,1:T(8,128)(2,1)}) fusion(f32[1024,1792]{0,1:T(8,128)} %bitcast.18, bf16[1024,1792]{0,1:T(8,128)(2,1)} %copy.24, f32[1024,1792]{0,1:T(8,128)} %bitcast.19, bf16[1024,1792]{0,1:T(8,128)(2,1)} %copy.22), kind=kLoop, calls=%fused_computation.5 | loop fusion | flops 11010048 | bytes 29360128 | tf_op jit(solution)/shard_map/convert_element_type | solution.py:15
  43.6 26.4 %all-gather.3.cloned.1.call-done = bf16[512,1024]{1,0:T(8,128)(2,1)} async-done(((bf16[32,1024]{1,0:T(8,128)(2,1)}), bf16[512,1024]{1,0:T(8,128)(2,1)}) %all-gather.3.cloned.1.call-update) | async-done | bytes 1048592 | tf_op jit(solution)/shard_map/all_gather | solution.py:26
  70.0 10.3 %fusion.4 = f32[512,3584]{0,1:T(8,128)} fusion(bf16[512,1024]{1,0:T(8,128)(2,1)} %all-gather.3.cloned.1.call-done, bf16[1024,1792]{0,1:T(8,128)(2,1)} %get-tuple-element.7, bf16[1024,1792]{0,1:T(8,128)(2,1)} %get-tuple-element.8), kind=kOutput, calls=%fused_computation.7 | convolution fusion | flops 3772776448 | bytes 15728640 | tf_op jit(solution)/shard_map/dot_general | solution.py:33
  80.3 8.4 %copy.29 = f32[512,3584]{1,0:T(8,128)} copy(f32[512,3584]{0,1:T(8,128)} %fusion.4) | data formatting | bytes 14680064
  88.7 0.0 copy-start
  88.7 0.0 copy-start.1
  88.7 0.0 reduce-scatter.7.cloned.1.call-update
  88.8 0.0 all-gather.5.cloned.1.call-start
  88.8 159.9 %reduce-scatter.7.cloned.1.call-done = f32[32,3584]{1,0:T(8,128)} async-done(((f32[512,3584]{1,0:T(8,128)}), f32[32,3584]{1,0:T(8,128)}) %reduce-scatter.7.cloned.1.call-update) | async-done | bytes 458768 | tf_op jit(solution)/shard_map/reduce_scatter | solution.py:32
  248.8 1.8 fusion.8
  250.5 0.0 all-gather.5.cloned.1.call-update
  250.5 0.0 reduce-scatter.5.cloned.1.call-start
  250.6 0.0 copy-done
  250.6 0.0 copy-done.1
  250.6 0.1 copy.28
  250.7 1.0 mul.60
  251.7 4.7 %copy.33 = f32[224,8,4,256]{3,1,2,0:T(8,128)} copy(f32[224,8,4,256]{3,2,1,0:T(4,128)S(1)} %bitcast.23) | data formatting | bytes 14680064
  256.5 68.6 %all-gather.5.cloned.1.call-done = bf16[512,1792]{1,0:T(8,128)(2,1)} async-done(((bf16[32,1792]{1,0:T(8,128)(2,1)}), bf16[512,1792]{1,0:T(8,128)(2,1)}) %all-gather.5.cloned.1.call-update) | async-done | bytes 1835024 | tf_op jit(solution)/shard_map/all_gather | solution.py:39
  325.1 8.1 %fusion.7 = f32[512,1024]{1,0:T(8,128)} fusion(bf16[512,1792]{1,0:T(8,128)(2,1)} %all-gather.5.cloned.1.call-done, f32[1792,1024]{1,0:T(8,128)} %bitcast.20, bf16[1792,1024]{1,0:T(8,128)(2,1)} %param.15), kind=kOutput, calls=%fused_computation.8 | convolution fusion | flops 1884553216 | bytes 14942208 | tf_op jit(solution)/shard_map/dot_general | solution.py:43
  333.2 0.0 reduce-scatter.5.cloned.1.call-update
  333.2 94.8 %reduce-scatter.5.cloned.1.call-done = f32[32,1024]{1,0:T(8,128)} async-done(((f32[512,1024]{1,0:T(8,128)}), f32[32,1024]{1,0:T(8,128)}) %reduce-scatter.5.cloned.1.call-update) | async-done | bytes 131088 | tf_op jit(solution)/shard_map/reduce_scatter | solution.py:42
  428.1 1.5 convert_element_type.40
  (1 shorter events, 0.0 us)
Async XLA Ops:
  6.5 63.4 %all-gather.3.cloned.1.call-start = ((), (), s32[]{:S(2)}) async-start(), calls=%async_computation.2 | async-start | bytes 1114112 | tf_op jit(solution)/shard_map/all_gather | solution.py:26
  7.3 241.5 %reduce-scatter.7.cloned.1.call-start = ((), (), s32[]{:S(2)}) async-start(), calls=%async_computation.5 | async-start | bytes 7798784 | tf_op jit(solution)/shard_map/reduce_scatter | solution.py:32
  88.7 161.8 %copy-start = (f32[7,4]{0,1:T(4,128)S(1)}, f32[7,4]{0,1:T(4,128)}, u32[]{:S(2)}) copy-start(f32[7,4]{0,1:T(4,128)} %param.16) | copy-start | bytes 340
  88.7 161.9 %copy-start.1 = (s32[7,4]{0,1:T(4,128)S(1)}, s32[7,4]{0,1:T(4,128)}, u32[]{:S(2)}) copy-start(s32[7,4]{0,1:T(4,128)} %param.17) | copy-start | bytes 340
  88.8 236.3 %all-gather.5.cloned.1.call-start = ((), (), s32[]{:S(2)}) async-start(), calls=%async_computation.3 | async-start | bytes 1949696 | tf_op jit(solution)/shard_map/all_gather | solution.py:39
  250.5 177.5 %reduce-scatter.5.cloned.1.call-start = ((), (), s32[]{:S(2)}) async-start(), calls=%async_computation.4 | async-start | bytes 2228224 | tf_op jit(solution)/shard_map/reduce_scatter | solution.py:42
Sparse Core Ops, SparseCore 0:
  10.0 59.8 all-gather.2
  88.9 159.8 reduce-scatter.6
  250.7 74.3 all-gather.4
  333.4 94.6 reduce-scatter.4
where the time goes:
time: 437 us; the launch traced here: 436 us
  waiting for transfers between devices  351 us (80%)
  local copies, waits for them, and re-layouts  38 us (9%)
  matrix products  18.5 us (4%)
  other arithmetic  15.8 us (4%)
  between operations  13.2 us (3%)
    reduce_scatter x1, waiting for transfers between devices, per_device(): lax.psum_scatter(jnp.dot(rows, weight_both, preferred_element_type=jnp.fl...  160 us
    reduce_scatter x1, waiting for transfers between devices, per_device(): lax.psum_scatter(jnp.dot(rows, weight_down, preferred_element_type=jnp.fl...  94.8 us
    all_gather x1, waiting for transfers between devices, per_device(): hidden_all = lax.all_gather(hidden, 'row', axis=0, tiled=True)  68.6 us
    unnamed x10, local copies, waits for them, and re-layouts  34.7 us
    all_gather x1, waiting for transfers between devices, per_device(): panel = lax.all_gather(tokens, 'col', axis=0, tiled=True)  26.4 us
    convert_element_type x1, other arithmetic, dequantize(): return values.reshape(rows, cols).astype(jnp.bfloat16)  11.8 us
    dot_general x1, matrix products, per_device(): jnp.dot(rows, weight_both, preferred_element_type=jnp.float32)  10.3 us
  transfers between devices with their start and end apart: 4, of which 4 were waited for; matrix products, arithmetic and copies ran while one was open for 10% of the time, Pallas kernels for 0%

commit v1 on v0

v1 whole, which is shorter than its diff:
```python
import functools

import jax
import jax.numpy as jnp
from jax import lax
from jax.experimental import pallas as pl
from jax.experimental.pallas import tpu as pltpu
from jax.sharding import PartitionSpec as P

MESH = pl.DeviceIdType.MESH
F32 = jnp.float32
BF16 = jnp.bfloat16

X, ZL, Y, ZH, CORES = 4, 4, 4, 2, 2
GROUPS = Y
HOPS = (0, 2, 1, 3)


def kernel(
    tokens_hbm, gate_hbm, gate_scale, up_hbm, up_scale, gate_keep, down_hbm, down_scale, down_keep,
    out_ref,
    panel, w1, w2, part, relay, near, zsend, zrecv, hid, prod, sib, ysend, yrecv, own, hsend, hrecv,
    load_sem, ay_send, ay_recv, az_send, az_recv, as_send, as_recv,
    b_send, b_recv, z_send, z_recv, hz_send, hz_recv, hx_send, hx_recv,
    ds_send, ds_recv, dy_send, dy_recv, dz_send, dz_recv,
):
    rows, depth = tokens_hbm.shape
    width = gate_hbm.shape[1]
    half = width // 2
    tile = depth // gate_scale.shape[0]
    small = rows // 2

    row, col = lax.axis_index("row"), lax.axis_index("col")
    x, zl = row // ZL, row % ZL
    y, zh, core = col // (ZH * CORES), (col // CORES) % ZH, col % CORES

    def at_x(d):
        return (((x + d) % X) * ZL + zl, col)

    def at_zl(d):
        return (x * ZL + (zl + d) % ZL, col)

    def at_y(d):
        return (row, (((y + d) % Y) * ZH + zh) * CORES + core)

    across = (row, (y * ZH + (1 - zh)) * CORES + core)
    sibling = (row, (y * ZH + zh) * CORES + (1 - core))

    def remote(src, dst, send, recv, to):
        return pltpu.make_async_remote_copy(
            src_ref=src, dst_ref=dst, send_sem=send, recv_sem=recv, device_id=to, device_id_type=MESH
        )

    started = []

    def go(src, dst, send, recv, to):
        copy = remote(src, dst, send, recv, to)
        copy.start()
        started.append(copy)

    def arrive(dst, send, recv):
        remote(dst, dst, send, recv, sibling).wait_recv()

    my_block = panel.at[y, pl.ds(pl.multiple_of((zh * CORES + core) * rows, rows), rows)]
    load_tokens = pltpu.make_async_copy(tokens_hbm, my_block, load_sem.at[0])
    load_tokens.start()
    loads = []
    for u in range(2):
        for p, codes in enumerate((gate_hbm, up_hbm)):
            load = pltpu.make_async_copy(
                codes.at[:, pl.ds(u * half, half)],
                w1.at[u, :, pl.ds(p * half, half)],
                load_sem.at[1 + 2 * u + p],
            )
            load.start()
            loads.append(load)
    load_down = pltpu.make_async_copy(down_hbm, w2, load_sem.at[5])
    load_down.start()

    barrier = pltpu.get_barrier_semaphore()
    peers = [at_x(1), at_x(3), at_zl(1), at_zl(2), at_zl(3), at_y(1), at_y(2), at_y(3), across, sibling]
    for peer in peers:
        pl.semaphore_signal(barrier, inc=1, device_id=peer, device_id_type=MESH)
    pl.semaphore_wait(barrier, len(peers))

    def block(s, d):
        j = ((zh + s) % ZH) * CORES + core
        return panel.at[(y + d) % Y, pl.ds(pl.multiple_of(j * rows, rows), rows)]

    def sibling_block(s, d):
        j = ((zh + s) % ZH) * CORES + (1 - core)
        return panel.at[(y + d) % Y, pl.ds(pl.multiple_of(j * rows, rows), rows)]

    def to_sibling(s, d):
        b = block(s, d)
        go(b, b, as_send.at[s, d], as_recv.at[s, d], sibling)

    def to_columns(s):
        b = block(s, 0)
        for d in (2, 1, 3):
            go(b, b, ay_send.at[s, d], ay_recv.at[s, d], at_y(d))

    def tokens_first():
        load_tokens.wait()
        go(my_block, my_block, az_send, az_recv, across)
        to_sibling(0, 0)
        to_columns(0)

    def tokens_across():
        arrive(block(1, 0), az_send, az_recv)
        to_sibling(1, 0)
        to_columns(1)

    def tokens_of(d):
        if d:
            for s in range(2):
                back = (Y - d) % Y
                arrive(block(s, d), ay_send.at[s, back], ay_recv.at[s, back])
                to_sibling(s, d)
        for s in range(2):
            arrive(sibling_block(s, d), as_send.at[s, d], as_recv.at[s, d])

    def dequant1(u):
        for p, scale in enumerate((gate_scale, up_scale)):
            loads[2 * u + p].wait()

            @pl.loop(0, half // 128)
            def _(s):
                at = pl.ds(pl.multiple_of(p * half + s * 128, 128), 128)
                j = (u * (half // 128) + s) // (tile // 128)
                for i in range(depth // tile):
                    factor = scale[i, j] * gate_keep[i, j].astype(F32)
                    here = pl.ds(i * tile, tile)
                    w1[u, here, at] = (w1[u, here, at].astype(F32) * factor).astype(BF16)

    def dequant2():
        load_down.wait()

        @pl.loop(0, width // tile)
        def _(i):
            here = pl.ds(pl.multiple_of(i * tile, tile), tile)
            for j in range(depth // tile):
                factor = down_scale[j, i] * down_keep[j, i].astype(F32)
                at = pl.ds(j * tile, tile)
                w2[here, at] = (w2[here, at].astype(F32) * factor).astype(BF16)

    def block_rows(d):
        return pl.ds(pl.multiple_of(((x + d) % X) * rows, rows), rows)

    def product(g, u):
        yy = (y + HOPS[g]) % Y

        @pl.loop(0, width // 256)
        def _(n):
            at = pl.ds(pl.multiple_of(n * 256, 256), 256)
            part[g, u, :, at] = jnp.dot(
                panel[yy], w1[u, :, at], preferred_element_type=F32
            ).astype(BF16)

        on, plain = (1, 3) if u == 0 else (3, 1)
        go(part.at[g, u, block_rows(2)], relay.at[g, u], b_send.at[g, u, 0], b_recv.at[g, u, 0], at_x(on))
        go(part.at[g, u, block_rows(plain)], near.at[g, 1, u], b_send.at[g, u, 1], b_recv.at[g, u, 1], at_x(plain))

    def merge(g):
        for u in range(2):
            arrive(relay.at[g, u], b_send.at[g, u, 0], b_recv.at[g, u, 0])
            on = 1 if u == 0 else 3
            here = block_rows(on)
            part[g, u, here, :] = (part[g, u, here, :].astype(F32) + relay[g, u].astype(F32)).astype(BF16)
            go(part.at[g, u, here], near.at[g, 0, u], b_send.at[g, u, 2], b_recv.at[g, u, 2], at_x(on))

    mine_h, mine_u = zl // 2, zl % 2

    def sum_x(g):
        for u in range(2):
            arrive(near.at[g, 1, u], b_send.at[g, u, 1], b_recv.at[g, u, 1])
            arrive(near.at[g, 0, u], b_send.at[g, u, 2], b_recv.at[g, u, 2])
            zsend[g, u] = (
                part[g, u, block_rows(0), :].astype(F32) + near[g, 0, u].astype(F32) + near[g, 1, u].astype(F32)
            ).astype(BF16)
        for d in (2, 1, 3):
            to = (zl + d) % ZL
            go(
                zsend.at[g, to % 2, pl.ds(pl.multiple_of((to // 2) * small, small), small)],
                zrecv.at[g, d - 1], z_send.at[g, d - 1], z_recv.at[g, d - 1], at_zl(d),
            )

    def piece(z):
        return (
            pl.ds(pl.multiple_of(x * rows + (z // 2) * small, small), small),
            pl.ds(pl.multiple_of((z % 2) * half, 128), half),
        )

    def activate(g):
        for d in (1, 2, 3):
            arrive(zrecv.at[g, d - 1], z_send.at[g, d - 1], z_recv.at[g, d - 1])
        in_block = pl.ds(pl.multiple_of(mine_h * small, small), small)
        in_group = pl.ds(pl.multiple_of(x * rows + mine_h * small, small), small)

        def total(at):
            t = part[g, mine_u, in_group, at].astype(F32)
            t += near[g, 0, mine_u, in_block, at].astype(F32) + near[g, 1, mine_u, in_block, at].astype(F32)
            for d in range(3):
                t += zrecv[g, d, :, at].astype(F32)
            return t

        gate, up = total(pl.ds(0, half)), total(pl.ds(half, half))
        at_rows, at_cols = piece(zl)
        hid[g, at_rows, at_cols] = (gate / (1.0 + jnp.exp(-gate)) * up).astype(BF16)
        for d in (2, 1, 3):
            there = hid.at[g, at_rows, at_cols]
            go(there, there, hz_send.at[g, d - 1], hz_recv.at[g, d - 1], at_zl(d))

    def spread(g):
        for d in (1, 2, 3):
            at_rows, at_cols = piece((zl + ZL - d) % ZL)
            arrive(hid.at[g, at_rows, at_cols], hz_send.at[g, d - 1], hz_recv.at[g, d - 1])
        there = hid.at[g, block_rows(0)]
        go(there, there, hx_send.at[g, 0], hx_recv.at[g, 0], at_x(1))
        go(there, there, hx_send.at[g, 1], hx_recv.at[g, 1], at_x(3))

    def forward(g):
        for k, (source, to) in enumerate(((3, 1), (1, 3))):
            arrive(hid.at[g, block_rows(source)], hx_send.at[g, k], hx_recv.at[g, k])
            there = hid.at[g, block_rows(source), pl.ds(k * half, half)]
            go(there, there, hx_send.at[g, 2 + k], hx_recv.at[g, 2 + k], at_x(to))

    def down(g):
        for k in range(2):
            there = hid.at[g, block_rows(2), pl.ds(k * half, half)]
            arrive(there, hx_send.at[g, 2 + k], hx_recv.at[g, 2 + k])

        @pl.loop(0, depth // 256)
        def _(n):
            at = pl.ds(pl.multiple_of(n * 256, 256), 256)
            prod[g, :, :, at] = jnp.dot(
                hid[g], w2[:, at], preferred_element_type=F32
            ).reshape(ZH * CORES, rows, 256)

        for z in range(2):
            go(prod.at[g, z * CORES + (1 - core)], sib.at[g, z], ds_send.at[g, z], ds_recv.at[g, z], sibling)

    def to_owner(g):
        for z in range(2):
            arrive(sib.at[g, z], ds_send.at[g, z], ds_recv.at[g, z])
            s = prod[g, z * CORES + core] + sib[g, z]
            if HOPS[g]:
                ysend[g, z] = s.astype(BF16)
            else:
                own[z] = s
        if HOPS[g]:
            go(ysend.at[g], yrecv.at[g], dy_send.at[g], dy_recv.at[g], at_y(HOPS[g]))

    def finish():
        for g in range(GROUPS):
            if HOPS[g]:
                arrive(yrecv.at[g], dy_send.at[g], dy_recv.at[g])

        def total(z):
            t = own[z]
            for g in range(GROUPS):
                if HOPS[g]:
                    t += yrecv[g, z].astype(F32)
            return t

        hsend[...] = total(1 - zh).astype(BF16)
        go(hsend, hrecv, dz_send, dz_recv, across)
        kept = total(zh)
        arrive(hrecv, dz_send, dz_recv)
        out_ref[...] = (kept + hrecv[...].astype(F32)).astype(BF16)

    tokens_first()
    dequant1(0)
    tokens_across()
    dequant1(1)
    for t in range(GROUPS + 4):
        if t < GROUPS:
            tokens_of(HOPS[t])
            product(t, 0)
            product(t, 1)
        if t == 0:
            dequant2()
        if 0 <= t - 2 < GROUPS:
            activate(t - 2)
        if t < GROUPS:
            merge(t)
        if 0 <= t - 1 < GROUPS:
            sum_x(t - 1)
        if 0 <= t - 2 < GROUPS:
            spread(t - 2)
        if 0 <= t - 3 < GROUPS:
            forward(t - 3)
            down(t - 3)
        if 0 <= t - 4 < GROUPS:
            to_owner(t - 4)
    finish()
    for copy in started:
        copy.wait_send()


def per_device(
    tokens, gate_codes, gate_scale, up_codes, up_scale, gate_keep, down_codes, down_scale, down_keep
):
    rows, depth = tokens.shape
    width = gate_codes.shape[1]
    half, small, group = width // 2, rows // 2, rows * ZH * CORES
    hbm = pl.BlockSpec(memory_space=pl.ANY)
    smem = pl.BlockSpec(memory_space=pltpu.SMEM)
    dma = pltpu.SemaphoreType.DMA
    G = GROUPS
    return pl.pallas_call(
        kernel,
        out_shape=jax.ShapeDtypeStruct((rows, depth), BF16),
        in_specs=[hbm, hbm, smem, hbm, smem, smem, hbm, smem, smem],
        out_specs=pl.BlockSpec(memory_space=pltpu.VMEM),
        scratch_shapes=[
            pltpu.VMEM((Y, group, depth), BF16),
            pltpu.VMEM((2, depth, width), BF16),
            pltpu.VMEM((width, depth), BF16),
            pltpu.VMEM((G, 2, group, width), BF16),
            pltpu.VMEM((G, 2, rows, width), BF16),
            pltpu.VMEM((G, 2, 2, rows, width), BF16),
            pltpu.VMEM((G, 2, rows, width), BF16),
            pltpu.VMEM((G, ZL - 1, small, width), BF16),
            pltpu.VMEM((G, group, width), BF16),
            pltpu.VMEM((G, ZH * CORES, rows, depth), F32),
            pltpu.VMEM((G, ZH, rows, depth), F32),
            pltpu.VMEM((G, ZH, rows, depth), BF16),
            pltpu.VMEM((G, ZH, rows, depth), BF16),
            pltpu.VMEM((ZH, rows, depth), F32),
            pltpu.VMEM((rows, depth), BF16),
            pltpu.VMEM((rows, depth), BF16),
            dma((6,)),
            dma((2, Y)), dma((2, Y)),
            dma(()), dma(()),
            dma((2, Y)), dma((2, Y)),
            dma((G, 2, 3)), dma((G, 2, 3)),
            dma((G, 3)), dma((G, 3)),
            dma((G, 3)), dma((G, 3)),
            dma((G, 4)), dma((G, 4)),
            dma((G, 2)), dma((G, 2)),
            dma((G,)), dma((G,)),
            dma(()), dma(()),
        ],
        compiler_params=pltpu.CompilerParams(
            collective_id=0, has_side_effects=True, vmem_limit_bytes=56 * 1024 * 1024
        ),
    )(tokens, gate_codes, gate_scale, up_codes, up_scale, gate_keep, down_codes, down_scale.T, down_keep.T)


def solution(mesh):
    placed = (
        P("col", "row"),
        P("row", "col"),
        P("row", "col"),
        P("row", "col"),
        P("row", "col"),
        P("row", "col"),
        P("col", "row"),
        P("col", "row"),
        P("col", "row"),
    )
    return jax.shard_map(
        per_device, mesh=mesh, in_specs=placed, out_specs=P("col", "row"), check_vma=False
    )
```

time: 437 us -> 110 us (0.25)
  waiting for transfers between devices: 351 us -> 0 us
  Pallas kernels: 0 us -> 108 us
  local copies, waits for them, and re-layouts: 38 us -> 1.47 us
  matrix products: 18.5 us -> 0 us
  other arithmetic: 15.8 us -> 0 us
  between operations: 13.2 us -> 0.01 us
    reduce_scatter x2 -> x0, waiting for transfers between devices: 255 us -> none  [the longest x1 160 us: per_device(): lax.psum_scatter(jnp.dot(rows, weight_both, preferred_element_type=jnp.fl...]
    pallas_call x0 -> x1, Pallas kernels: none -> 108 us  [per_device(): pl.pallas_call(kernel, out_shape=jax.ShapeDtypeStruct((rows, depth), BF16...]
    all_gather x2 -> x0, waiting for transfers between devices: 95 us -> none  [the longest x1 68.6 us: per_device(): hidden_all = lax.all_gather(hidden, 'row', axis=0, tiled=True)]
    unnamed x10 -> x1, local copies, waits for them, and re-layouts: 34.7 us -> 1.47 us
    dot_general x2 -> x0, matrix products: 18.5 us -> none  [the longest x1 10.3 us: per_device(): jnp.dot(rows, weight_both, preferred_element_type=jnp.float32)]
    convert_element_type x3 -> x0, other arithmetic: 15.1 us -> none  [the longest x1 11.8 us: dequantize(): return values.reshape(rows, cols).astype(jnp.bfloat16)]
  transfers between devices with their start and end apart: 4 -> 0, of which waited for: 4 -> 0; matrix products, arithmetic and copies ran while one was open for 10% -> 0% of each run, Pallas kernels for 0% -> 0%
where the time goes in v1:
time: 110 us; the launch traced here: 109 us
  Pallas kernels  108 us (98%)
  local copies, waits for them, and re-layouts  1.47 us (1%)
    pallas_call x1, Pallas kernels, per_device(): pl.pallas_call(kernel, out_shape=jax.ShapeDtypeStruct((rows, depth), BF16...  108 us

profile of v1, /device:TPU:1, one launch (start us, length us, event | category | flops | bytes accessed | tf_op | source)
XLA Modules:
  0.0 109.1 jit_solution(18170010703273246209)
XLA Ops:
  0.0 107.6 %shard_map.91 = bf16[32,1024]{1,0:T(8,128)(2,1)} custom-call(bf16[32,1024]{1,0:T(8,128)(2,1)} %tokens_hbm.1, bf16[1024,1792]{1,0:T(8,128)(2,1)} %gate_hbm.1, f32[4,7]{1,0:T(4,128)} %gate_scale.1, bf16[1024,1792]{1,0:T(8,128)(2,1)} %up_hbm.1, f32[4,7]{1,0:T(4,128)} %up_scale.1, s32[4,7]{1,0:T(4,128)} %gate_keep.1, bf16[1792,1024]{1,0:T(8,128)(2,1)} %down_hbm.1, ...), custom_call_target="tpu_custom_call" | custom-call | tf_op jit(solution)/shard_map/pallas_call | solution.py:311
  107.6 1.5 %copy.11 = bf16[32,1024]{1,0:T(8,128)(2,1)} copy(bf16[32,1024]{1,0:T(8,128)(2,1)} %shard_map.91) | data formatting | bytes 131072

commit v2 on v0

v2 whole, which is shorter than its diff:
```python
import jax
import jax.numpy as jnp
from jax import lax
from jax.experimental import pallas as pl
from jax.experimental.pallas import tpu as pltpu
from jax.sharding import PartitionSpec as P

MESH = pl.DeviceIdType.MESH
F32 = jnp.float32
BF16 = jnp.bfloat16
LANES = 128

X, ZL, Y, ZH, CORES = 4, 4, 4, 2, 2
UNITS = ((1, 0), (3, 0), (2, 0), (1, 1), (3, 1), (2, 1), (0, 1), (0, 0))
N = len(UNITS)
SLOT = {unit: i for i, unit in enumerate(UNITS)}


def kernel(
    tokens_hbm, gate_hbm, gate_scale, up_hbm, up_scale, gate_keep, down_hbm, down_scale, down_keep,
    out_ref,
    panel, raw, w1, w2, acc, part, relay, near, xsum, zsend, zrecv, hid, prod, sib, ysend, yrecv, own, hsend, hrecv,
    load_sem, ay_send, ay_recv, az_send, az_recv, as_send, as_recv,
    b_send, b_recv, z_send, z_recv, hz_send, hz_recv, hx_send, hx_recv,
    ds_send, ds_recv, dy_send, dy_recv, dz_send, dz_recv,
):
    rows, depth = tokens_hbm.shape
    width = gate_hbm.shape[1]
    tile = depth // gate_scale.shape[0]
    small = rows * CORES // X
    pairs = width // LANES
    share = -(-pairs // ZL)
    piece, hpiece = share * 2 * LANES, share * LANES

    row, col = lax.axis_index("row"), lax.axis_index("col")
    x, zl = row // ZL, row % ZL
    y, zh, core = col // (ZH * CORES), (col // CORES) % ZH, col % CORES

    def at_x(d):
        return (((x + d) % X) * ZL + zl, col)

    def at_zl(d):
        return (x * ZL + (zl + d) % ZL, col)

    def at_y(d):
        return (row, (((y + d) % Y) * ZH + zh) * CORES + core)

    across = (row, (y * ZH + (1 - zh)) * CORES + core)
    sibling = (row, (y * ZH + zh) * CORES + (1 - core))

    def remote(src, dst, send, recv, to):
        return pltpu.make_async_remote_copy(
            src_ref=src, dst_ref=dst, send_sem=send, recv_sem=recv, device_id=to, device_id_type=MESH
        )

    started = []

    def go(src, dst, send, recv, to):
        copy = remote(src, dst, send, recv, to)
        copy.start()
        started.append(copy)

    def arrive(dst, send, recv):
        remote(dst, dst, send, recv, sibling).wait_recv()

    def slot(d, s, c):
        return panel.at[SLOT[d, s], pl.ds(pl.multiple_of(c * rows, rows), rows)]

    mine = slot(0, 0, core)
    load_tokens = pltpu.make_async_copy(tokens_hbm, mine, load_sem.at[0])
    load_tokens.start()
    loads = []
    for p, codes in enumerate((gate_hbm, up_hbm)):
        load = pltpu.make_async_copy(codes, raw.at[p], load_sem.at[1 + p])
        load.start()
        loads.append(load)
    load_down = pltpu.make_async_copy(down_hbm, w2, load_sem.at[3])
    load_down.start()

    barrier = pltpu.get_barrier_semaphore()
    peers = [at_x(1), at_x(3), at_zl(1), at_zl(2), at_zl(3), at_y(1), at_y(2), at_y(3), across, sibling]
    for peer in peers:
        pl.semaphore_signal(barrier, inc=1, device_id=peer, device_id_type=MESH)
    pl.semaphore_wait(barrier, len(peers))

    def to_sibling(d, s):
        i = SLOT[d, s]
        go(slot(d, s, core), slot(d, s, core), as_send.at[i], as_recv.at[i], sibling)

    def to_columns(s):
        for d in (1, 3, 2):
            i = SLOT[d, s]
            go(slot(0, s, core), slot(d, s, core), ay_send.at[i], ay_recv.at[i], at_y(Y - d))

    def tokens_first():
        load_tokens.wait()
        to_columns(0)
        go(mine, slot(0, 1, core), az_send, az_recv, across)
        to_sibling(0, 0)

    def tokens_across():
        arrive(slot(0, 1, core), az_send, az_recv)
        to_columns(1)
        to_sibling(0, 1)

    def tokens_in(i):
        d, s = UNITS[i]
        if d:
            arrive(slot(d, s, core), ay_send.at[i], ay_recv.at[i])
            to_sibling(d, s)

    def tokens_all(i):
        d, s = UNITS[i]
        arrive(slot(d, s, 1 - core), as_send.at[i], as_recv.at[i])

    def dequant1():
        for load in loads:
            load.wait()

        @pl.loop(0, pairs)
        def _(t):
            j = t // (tile // LANES)
            at = pl.ds(pl.multiple_of(t * LANES, LANES), LANES)
            for p, scale in enumerate((gate_scale, up_scale)):
                to = pl.ds(pl.multiple_of(t * 2 * LANES + p * LANES, LANES), LANES)
                for i in range(depth // tile):
                    factor = scale[i, j] * gate_keep[i, j].astype(F32)
                    here = pl.ds(i * tile, tile)
                    w1[here, to] = (raw[p, here, at].astype(F32) * factor).astype(BF16)

    def dequant2():
        load_down.wait()

        @pl.loop(0, width // tile)
        def _(i):
            here = pl.ds(pl.multiple_of(i * tile, tile), tile)
            for j in range(depth // tile):
                factor = down_scale[j, i] * down_keep[j, i].astype(F32)
                at = pl.ds(j * tile, tile)
                w2[here, at] = (w2[here, at].astype(F32) * factor).astype(BF16)

    def block(d):
        return pl.ds(pl.multiple_of(((x + d) % X) * small, small), small)

    def cols(u):
        return pl.ds(u * width, width)

    def product(i):
        for u in range(2):
            t = jnp.dot(panel[i], w1[:, cols(u)], preferred_element_type=F32)
            acc[i, :, cols(u)] = t
            part[i, :, cols(u)] = t.astype(BF16)
            on, plain = (1, 3) if u == 0 else (3, 1)
            go(part.at[i, block(2), cols(u)], relay.at[i, u], b_send.at[i, u], b_recv.at[i, u], at_x(on))
            go(
                part.at[i, block(plain), cols(u)], near.at[i, 1, :, cols(u)],
                b_send.at[i, 2 + u], b_recv.at[i, 2 + u], at_x(plain),
            )

    def merge(i):
        for u in range(2):
            arrive(relay.at[i, u], b_send.at[i, u], b_recv.at[i, u])
            here = block(1 if u == 0 else 3)
            part[i, here, cols(u)] = (acc[i, here, cols(u)] + relay[i, u].astype(F32)).astype(BF16)
            go(
                part.at[i, here, cols(u)], near.at[i, 0, :, cols(u)],
                b_send.at[i, 4 + u], b_recv.at[i, 4 + u], at_x(1 if u == 0 else 3),
            )

    def sum_x(i):
        for u in range(2):
            arrive(near.at[i, 1, :, cols(u)], b_send.at[i, 2 + u], b_recv.at[i, 2 + u])
            arrive(near.at[i, 0, :, cols(u)], b_send.at[i, 4 + u], b_recv.at[i, 4 + u])
        both = pl.ds(0, 2 * width)
        t = acc[i, block(0), :] + near[i, 0].astype(F32) + near[i, 1].astype(F32)
        xsum[i, :, both] = t
        zsend[i, :, both] = t.astype(BF16)
        for d in (2, 1, 3):
            to = pl.multiple_of(((zl + d) % ZL) * piece, piece)
            go(
                zsend.at[i, :, pl.ds(to, piece)], zrecv.at[i, d - 1],
                z_send.at[i, d - 1], z_recv.at[i, d - 1], at_zl(d),
            )

    def hidden_piece(i, d):
        at = pl.multiple_of(((zl + d) % ZL) * hpiece, hpiece)
        return hid.at[i, block(0), pl.ds(at, hpiece)]

    def activate(i):
        for d in range(1, ZL):
            arrive(zrecv.at[i, d - 1], z_send.at[i, d - 1], z_recv.at[i, d - 1])
        t = xsum[i, :, pl.ds(pl.multiple_of(zl * piece, piece), piece)]
        for d in range(1, ZL):
            t += zrecv[i, d - 1].astype(F32)
        for p in range(share):
            gate = t[:, 2 * p * LANES : (2 * p + 1) * LANES]
            up = t[:, (2 * p + 1) * LANES : (2 * p + 2) * LANES]
            at = pl.ds(pl.multiple_of(zl * hpiece + p * LANES, LANES), LANES)
            hid[i, block(0), at] = (gate / (1.0 + jnp.exp(-gate)) * up).astype(BF16)
        here = hidden_piece(i, 0)
        for d in (2, 1, 3):
            go(here, here, hz_send.at[i, d - 1], hz_recv.at[i, d - 1], at_zl(d))

    def spread(i):
        for d in range(1, ZL):
            arrive(hidden_piece(i, ZL - d), hz_send.at[i, d - 1], hz_recv.at[i, d - 1])
        here = hid.at[i, block(0), pl.ds(0, width)]
        for k, d in enumerate((1, 3)):
            go(here, here, hx_send.at[i, k], hx_recv.at[i, k], at_x(d))

    def halves(k):
        return pl.ds(0, 2 * hpiece) if k == 0 else pl.ds(2 * hpiece, width - 2 * hpiece)

    def forward(i):
        for k, (source, to) in enumerate(((3, 1), (1, 3))):
            arrive(hid.at[i, block(source), pl.ds(0, width)], hx_send.at[i, k], hx_recv.at[i, k])
            here = hid.at[i, block(source), halves(k)]
            go(here, here, hx_send.at[i, 2 + k], hx_recv.at[i, 2 + k], at_x(to))

    def down(i):
        for k in range(2):
            arrive(hid.at[i, block(2), halves(k)], hx_send.at[i, 2 + k], hx_recv.at[i, 2 + k])
        t = jnp.dot(hid[i, :, pl.ds(0, width)], w2[...], preferred_element_type=F32)
        prod[i] = t.reshape(CORES, rows, depth)
        go(prod.at[i, 1 - core], sib.at[i], ds_send.at[i], ds_recv.at[i], sibling)

    def to_owner(i):
        d, s = UNITS[i]
        arrive(sib.at[i], ds_send.at[i], ds_recv.at[i])
        t = prod[i, core] + sib[i]
        if d:
            ysend[i] = t.astype(BF16)
            go(ysend.at[i], yrecv.at[i], dy_send.at[i], dy_recv.at[i], at_y(d))
        else:
            own[s] = t

    def total(s):
        t = own[s]
        for i, (d, ss) in enumerate(UNITS):
            if d and ss == s:
                arrive(yrecv.at[i], dy_send.at[i], dy_recv.at[i])
                t += yrecv[i].astype(F32)
        return t

    def cross():
        hsend[...] = total(1).astype(BF16)
        go(hsend, hrecv, dz_send, dz_recv, across)

    def finish():
        t = total(0)
        arrive(hrecv, dz_send, dz_recv)
        out_ref[...] = (t + hrecv[...].astype(F32)).astype(BF16)

    tokens_first()
    pad = pl.ds(2 * width, ZL * piece - 2 * width)
    for i in range(N):
        xsum[i, :, pad] = jnp.zeros((small, ZL * piece - 2 * width), F32)
        zsend[i, :, pad] = jnp.zeros((small, ZL * piece - 2 * width), BF16)
    dequant1()
    tokens_in(0)
    tokens_in(1)
    tokens_in(2)
    tokens_across()

    def at(i):
        return 0 <= i < N

    for t in range(N + 8):
        if at(t):
            tokens_all(t)
            product(t)
        if t == 0:
            for i in range(3, N):
                tokens_in(i)
        if t == 1:
            dequant2()
        if at(t - 1):
            merge(t - 1)
        if at(t - 2):
            sum_x(t - 2)
        if at(t - 3):
            activate(t - 3)
        if at(t - 4):
            spread(t - 4)
        if at(t - 5):
            forward(t - 5)
        if at(t - 6):
            down(t - 6)
        if at(t - 7):
            to_owner(t - 7)
            if t - 7 == SLOT[0, 1]:
                cross()
    finish()
    for copy in started:
        copy.wait_send()


def per_device(
    tokens, gate_codes, gate_scale, up_codes, up_scale, gate_keep, down_codes, down_scale, down_keep
):
    rows, depth = tokens.shape
    width = gate_codes.shape[1]
    unit, small = rows * CORES, rows * CORES // X
    share = -(-(width // LANES) // ZL)
    piece, hpiece = share * 2 * LANES, share * LANES
    hbm = pl.BlockSpec(memory_space=pl.ANY)
    smem = pl.BlockSpec(memory_space=pltpu.SMEM)
    vmem, dma = pltpu.VMEM, pltpu.SemaphoreType.DMA
    return pl.pallas_call(
        kernel,
        out_shape=jax.ShapeDtypeStruct((rows, depth), BF16),
        in_specs=[hbm, hbm, smem, hbm, smem, smem, hbm, smem, smem],
        out_specs=pl.BlockSpec(memory_space=pltpu.VMEM),
        scratch_shapes=[
            vmem((N, unit, depth), BF16),
            vmem((2, depth, width), BF16),
            vmem((depth, 2 * width), BF16),
            vmem((width, depth), BF16),
            vmem((N, unit, 2 * width), F32),
            vmem((N, unit, 2 * width), BF16),
            vmem((N, 2, small, width), BF16),
            vmem((N, 2, small, 2 * width), BF16),
            vmem((N, small, ZL * piece), F32),
            vmem((N, small, ZL * piece), BF16),
            vmem((N, ZL - 1, small, piece), BF16),
            vmem((N, unit, ZL * hpiece), BF16),
            vmem((N, CORES, rows, depth), F32),
            vmem((N, rows, depth), F32),
            vmem((N, rows, depth), BF16),
            vmem((N, rows, depth), BF16),
            vmem((ZH, rows, depth), F32),
            vmem((rows, depth), BF16),
            vmem((rows, depth), BF16),
            dma((4,)),
            dma((N,)), dma((N,)),
            dma(()), dma(()),
            dma((N,)), dma((N,)),
            dma((N, 6)), dma((N, 6)),
            dma((N, 3)), dma((N, 3)),
            dma((N, 3)), dma((N, 3)),
            dma((N, 4)), dma((N, 4)),
            dma((N,)), dma((N,)),
            dma((N,)), dma((N,)),
            dma(()), dma(()),
        ],
        compiler_params=pltpu.CompilerParams(
            collective_id=0, has_side_effects=True, vmem_limit_bytes=60 * 1024 * 1024
        ),
    )(tokens, gate_codes, gate_scale, up_codes, up_scale, gate_keep, down_codes, down_scale.T, down_keep.T)


def solution(mesh):
    placed = (
        P("col", "row"),
        P("row", "col"),
        P("row", "col"),
        P("row", "col"),
        P("row", "col"),
        P("row", "col"),
        P("col", "row"),
        P("col", "row"),
        P("col", "row"),
    )
    return jax.shard_map(
        per_device, mesh=mesh, in_specs=placed, out_specs=P("col", "row"), check_vma=False
    )
```

time: 437 us -> 87 us (0.20)
  the two profiles are of different devices: /device:TPU:1 before, /device:TPU:24 now
where the time goes in v2:
time: 87 us; the launch traced here: 86.9 us
  Pallas kernels  85.4 us (98%)
  local copies, waits for them, and re-layouts  1.47 us (2%)
    pallas_call x1, Pallas kernels, per_device(): pl.pallas_call(kernel, out_shape=jax.ShapeDtypeStruct((rows, depth), BF16...  85.4 us

profile of v2, /device:TPU:24, one launch (start us, length us, event | category | flops | bytes accessed | tf_op | source)
XLA Modules:
  0.0 86.9 jit_solution(13983812354576842011)
XLA Ops:
  0.0 85.4 %shard_map.91 = bf16[32,1024]{1,0:T(8,128)(2,1)} custom-call(bf16[32,1024]{1,0:T(8,128)(2,1)} %tokens_hbm.1, bf16[1024,1792]{1,0:T(8,128)(2,1)} %gate_hbm.1, f32[4,7]{1,0:T(4,128)} %gate_scale.1, bf16[1024,1792]{1,0:T(8,128)(2,1)} %up_hbm.1, f32[4,7]{1,0:T(4,128)} %up_scale.1, s32[4,7]{1,0:T(4,128)} %gate_keep.1, bf16[1792,1024]{1,0:T(8,128)(2,1)} %down_hbm.1, ...), custom_call_target="tpu_custom_call" | custom-call | tf_op jit(solution)/shard_map/pallas_call | solution.py:309
  85.4 1.5 %copy.11 = bf16[32,1024]{1,0:T(8,128)(2,1)} copy(bf16[32,1024]{1,0:T(8,128)(2,1)} %shard_map.91) | data formatting | bytes 131072

commit v3 on v2

--- a/solution.py
+++ b/solution.py
@@ -11,18 +11,24 @@
 LANES = 128
 
 X, ZL, Y, ZH, CORES = 4, 4, 4, 2, 2
-UNITS = ((1, 0), (3, 0), (2, 0), (1, 1), (3, 1), (2, 1), (0, 1), (0, 0))
+UNITS = ((1, 0), (3, 0), (0, 1), (1, 1), (3, 1), (2, 1), (2, 0), (0, 0))
 N = len(UNITS)
 SLOT = {unit: i for i, unit in enumerate(UNITS)}
+WARM = 18
+DIRECT = (6, 7)
+ORDER = (
+    "P7T0P0C0P2T1S7T3M0P3T4M2T5A7S0P4M3S2P5M4A0S3",
+    "P1T6A2M5S4X0X7S5M1A3P6A4A5S1X3X4S6X5D7F3F0A1",
+    "F4X2F5D3A6D4X1O3F2D0D5O4X6O5O0F1D2O2O7K0D6D1O6O1",
+)
 
 
 def kernel(
     tokens_hbm, gate_hbm, gate_scale, up_hbm, up_scale, gate_keep, down_hbm, down_scale, down_keep,
     out_ref,
     panel, raw, w1, w2, acc, part, relay, near, xsum, zsend, zrecv, hid, prod, sib, ysend, yrecv, own, hsend, hrecv,
-    load_sem, ay_send, ay_recv, az_send, az_recv, as_send, as_recv,
-    b_send, b_recv, z_send, z_recv, hz_send, hz_recv, hx_send, hx_recv,
-    ds_send, ds_recv, dy_send, dy_recv, dz_send, dz_recv,
+    load_sem, az_send, ay_send, as_send, b_send, z_send, hz_send, hx_send, ds_send, dy_send, dz_send,
+    az_recv, ay_recv, as_recv, relay_recv, near_recv, z_recv, hz_recv, hx_recv, hf_recv, ds_recv, dy_recv, dz_recv,
 ):
     rows, depth = tokens_hbm.shape
     width = gate_hbm.shape[1]
@@ -53,15 +59,14 @@
             src_ref=src, dst_ref=dst, send_sem=send, recv_sem=recv, device_id=to, device_id_type=MESH
         )
 
-    started = []
-
     def go(src, dst, send, recv, to):
-        copy = remote(src, dst, send, recv, to)
-        copy.start()
-        started.append(copy)
-
-    def arrive(dst, send, recv):
-        remote(dst, dst, send, recv, sibling).wait_recv()
+        remote(src, dst, send, recv, to).start()
+
+    def arrive(like, recv):
+        remote(like, like, az_send, recv, sibling).wait_recv()
+
+    def sent(like, send):
+        remote(like, like, send, az_recv, sibling).wait_send()
 
     def slot(d, s, c):
         return panel.at[SLOT[d, s], pl.ds(pl.multiple_of(c * rows, rows), rows)]
@@ -78,19 +83,19 @@
     load_down.start()
 
     barrier = pltpu.get_barrier_semaphore()
-    peers = [at_x(1), at_x(3), at_zl(1), at_zl(2), at_zl(3), at_y(1), at_y(2), at_y(3), across, sibling]
+    peers = [at_x(1), at_x(2), at_x(3), at_zl(1), at_zl(2), at_zl(3), at_y(1), at_y(2), at_y(3), across, sibling]
     for peer in peers:
         pl.semaphore_signal(barrier, inc=1, device_id=peer, device_id_type=MESH)
     pl.semaphore_wait(barrier, len(peers))
 
     def to_sibling(d, s):
         i = SLOT[d, s]
-        go(slot(d, s, core), slot(d, s, core), as_send.at[i], as_recv.at[i], sibling)
+        go(slot(d, s, core), slot(d, s, core), as_send, as_recv.at[i], sibling)
 
     def to_columns(s):
         for d in (1, 3, 2):
             i = SLOT[d, s]
-            go(slot(0, s, core), slot(d, s, core), ay_send.at[i], ay_recv.at[i], at_y(Y - d))
+            go(slot(0, s, core), slot(d, s, core), ay_send, ay_recv.at[i], at_y(Y - d))
 
     def tokens_first():
         load_tokens.wait()
@@ -99,19 +104,19 @@
         to_sibling(0, 0)
 
     def tokens_across():
-        arrive(slot(0, 1, core), az_send, az_recv)
+        arrive(slot(0, 1, core), az_recv)
         to_columns(1)
         to_sibling(0, 1)
 
     def tokens_in(i):
         d, s = UNITS[i]
         if d:
-            arrive(slot(d, s, core), ay_send.at[i], ay_recv.at[i])
+            arrive(slot(d, s, core), ay_recv.at[i])
             to_sibling(d, s)
 
     def tokens_all(i):
         d, s = UNITS[i]
-        arrive(slot(d, s, 1 - core), as_send.at[i], as_recv.at[i])
+        arrive(slot(d, s, 1 - core), as_recv.at[i])
 
     def dequant1():
         for load in loads:
@@ -146,40 +151,50 @@
         return pl.ds(u * width, width)
 
     def product(i):
+        tokens_all(i)
         for u in range(2):
             t = jnp.dot(panel[i], w1[:, cols(u)], preferred_element_type=F32)
             acc[i, :, cols(u)] = t
             part[i, :, cols(u)] = t.astype(BF16)
+            if i in DIRECT:
+                go(part.at[i, block(2), cols(u)], relay.at[i, u], b_send, near_recv.at[i], at_x(2))
+                for k, d in enumerate((1, 3)):
+                    go(part.at[i, block(d), cols(u)], near.at[i, k, :, cols(u)], b_send, near_recv.at[i], at_x(d))
+                continue
             on, plain = (1, 3) if u == 0 else (3, 1)
-            go(part.at[i, block(2), cols(u)], relay.at[i, u], b_send.at[i, u], b_recv.at[i, u], at_x(on))
+            go(part.at[i, block(2), cols(u)], relay.at[i, u], b_send, relay_recv.at[i, u], at_x(on))
             go(
                 part.at[i, block(plain), cols(u)], near.at[i, 1, :, cols(u)],
-                b_send.at[i, 2 + u], b_recv.at[i, 2 + u], at_x(plain),
+                b_send, near_recv.at[i], at_x(plain),
             )
 
     def merge(i):
         for u in range(2):
-            arrive(relay.at[i, u], b_send.at[i, u], b_recv.at[i, u])
+            arrive(relay.at[i, u], relay_recv.at[i, u])
             here = block(1 if u == 0 else 3)
             part[i, here, cols(u)] = (acc[i, here, cols(u)] + relay[i, u].astype(F32)).astype(BF16)
             go(
                 part.at[i, here, cols(u)], near.at[i, 0, :, cols(u)],
-                b_send.at[i, 4 + u], b_recv.at[i, 4 + u], at_x(1 if u == 0 else 3),
+                b_send, near_recv.at[i], at_x(1 if u == 0 else 3),
             )
 
     def sum_x(i):
+        if i in DIRECT:
+            arrive(part.at[i, pl.ds(0, 3 * small)], near_recv.at[i])
+        else:
+            arrive(near.at[i], near_recv.at[i])
         for u in range(2):
-            arrive(near.at[i, 1, :, cols(u)], b_send.at[i, 2 + u], b_recv.at[i, 2 + u])
-            arrive(near.at[i, 0, :, cols(u)], b_send.at[i, 4 + u], b_recv.at[i, 4 + u])
-        both = pl.ds(0, 2 * width)
-        t = acc[i, block(0), :] + near[i, 0].astype(F32) + near[i, 1].astype(F32)
-        xsum[i, :, both] = t
-        zsend[i, :, both] = t.astype(BF16)
+            at = cols(u)
+            t = acc[i, block(0), at] + near[i, 0, :, at].astype(F32) + near[i, 1, :, at].astype(F32)
+            if i in DIRECT:
+                t += relay[i, u].astype(F32)
+            xsum[i, :, at] = t
+            zsend[i, :, at] = t.astype(BF16)
         for d in (2, 1, 3):
             to = pl.multiple_of(((zl + d) % ZL) * piece, piece)
             go(
                 zsend.at[i, :, pl.ds(to, piece)], zrecv.at[i, d - 1],
-                z_send.at[i, d - 1], z_recv.at[i, d - 1], at_zl(d),
+                z_send, z_recv.at[i], at_zl(d),
             )
 
     def hidden_piece(i, d):
@@ -187,8 +202,7 @@
         return hid.at[i, block(0), pl.ds(at, hpiece)]
 
     def activate(i):
-        for d in range(1, ZL):
-            arrive(zrecv.at[i, d - 1], z_send.at[i, d - 1], z_recv.at[i, d - 1])
+        arrive(zrecv.at[i], z_recv.at[i])
         t = xsum[i, :, pl.ds(pl.multiple_of(zl * piece, piece), piece)]
         for d in range(1, ZL):
             t += zrecv[i, d - 1].astype(F32)
@@ -199,38 +213,39 @@
             hid[i, block(0), at] = (gate / (1.0 + jnp.exp(-gate)) * up).astype(BF16)
         here = hidden_piece(i, 0)
         for d in (2, 1, 3):
-            go(here, here, hz_send.at[i, d - 1], hz_recv.at[i, d - 1], at_zl(d))
+            go(here, here, hz_send, hz_recv.at[i], at_zl(d))
 
     def spread(i):
-        for d in range(1, ZL):
-            arrive(hidden_piece(i, ZL - d), hz_send.at[i, d - 1], hz_recv.at[i, d - 1])
+        arrive(hid.at[i, block(0), pl.ds(0, (ZL - 1) * hpiece)], hz_recv.at[i])
         here = hid.at[i, block(0), pl.ds(0, width)]
-        for k, d in enumerate((1, 3)):
-            go(here, here, hx_send.at[i, k], hx_recv.at[i, k], at_x(d))
+        for d in (2, 1, 3) if i in DIRECT else (1, 3):
+            go(here, here, hx_send, hx_recv.at[i], at_x(d))
 
     def halves(k):
         return pl.ds(0, 2 * hpiece) if k == 0 else pl.ds(2 * hpiece, width - 2 * hpiece)
 
     def forward(i):
+        arrive(hid.at[i, pl.ds(0, 2 * small), pl.ds(0, width)], hx_recv.at[i])
         for k, (source, to) in enumerate(((3, 1), (1, 3))):
-            arrive(hid.at[i, block(source), pl.ds(0, width)], hx_send.at[i, k], hx_recv.at[i, k])
             here = hid.at[i, block(source), halves(k)]
-            go(here, here, hx_send.at[i, 2 + k], hx_recv.at[i, 2 + k], at_x(to))
+            go(here, here, hx_send, hf_recv.at[i], at_x(to))
 
     def down(i):
-        for k in range(2):
-            arrive(hid.at[i, block(2), halves(k)], hx_send.at[i, 2 + k], hx_recv.at[i, 2 + k])
+        if i in DIRECT:
+            arrive(hid.at[i, pl.ds(0, 3 * small), pl.ds(0, width)], hx_recv.at[i])
+        else:
+            arrive(hid.at[i, block(2), pl.ds(0, width)], hf_recv.at[i])
         t = jnp.dot(hid[i, :, pl.ds(0, width)], w2[...], preferred_element_type=F32)
         prod[i] = t.reshape(CORES, rows, depth)
-        go(prod.at[i, 1 - core], sib.at[i], ds_send.at[i], ds_recv.at[i], sibling)
+        go(prod.at[i, 1 - core], sib.at[i], ds_send, ds_recv.at[i], sibling)
 
     def to_owner(i):
         d, s = UNITS[i]
-        arrive(sib.at[i], ds_send.at[i], ds_recv.at[i])
+        arrive(sib.at[i], ds_recv.at[i])
         t = prod[i, core] + sib[i]
         if d:
             ysend[i] = t.astype(BF16)
-            go(ysend.at[i], yrecv.at[i], dy_send.at[i], dy_recv.at[i], at_y(d))
+            go(ysend.at[i], yrecv.at[i], dy_send, dy_recv.at[i], at_y(d))
         else:
             own[s] = t
 
@@ -238,7 +253,7 @@
         t = own[s]
         for i, (d, ss) in enumerate(UNITS):
             if d and ss == s:
-                arrive(yrecv.at[i], dy_send.at[i], dy_recv.at[i])
+                arrive(yrecv.at[i], dy_recv.at[i])
                 t += yrecv[i].astype(F32)
         return t
 
@@ -248,7 +263,7 @@
 
     def finish():
         t = total(0)
-        arrive(hrecv, dz_send, dz_recv)
+        arrive(hrecv, dz_recv)
         out_ref[...] = (t + hrecv[...].astype(F32)).astype(BF16)
 
     tokens_first()
@@ -257,42 +272,26 @@
         xsum[i, :, pad] = jnp.zeros((small, ZL * piece - 2 * width), F32)
         zsend[i, :, pad] = jnp.zeros((small, ZL * piece - 2 * width), BF16)
     dequant1()
-    tokens_in(0)
-    tokens_in(1)
-    tokens_in(2)
-    tokens_across()
-
-    def at(i):
-        return 0 <= i < N
-
-    for t in range(N + 8):
-        if at(t):
-            tokens_all(t)
-            product(t)
-        if t == 0:
-            for i in range(3, N):
-                tokens_in(i)
-        if t == 1:
+    stages = {
+        "T": tokens_in, "C": lambda _: tokens_across(), "P": product, "M": merge, "S": sum_x, "A": activate,
+        "X": spread, "F": forward, "D": down, "O": to_owner, "K": lambda _: cross(),
+    }
+    order = "".join(ORDER)
+    for k in range(0, len(order), 2):
+        stages[order[k]](int(order[k + 1]))
+        if k == WARM:
             dequant2()
-        if at(t - 1):
-            merge(t - 1)
-        if at(t - 2):
-            sum_x(t - 2)
-        if at(t - 3):
-            activate(t - 3)
-        if at(t - 4):
-            spread(t - 4)
-        if at(t - 5):
-            forward(t - 5)
-        if at(t - 6):
-            down(t - 6)
-        if at(t - 7):
-            to_owner(t - 7)
-            if t - 7 == SLOT[0, 1]:
-                cross()
     finish()
-    for copy in started:
-        copy.wait_send()
+    sent(mine, az_send)
+    sent(panel.at[pl.ds(0, 3)], ay_send)
+    sent(panel.at[pl.ds(0, 4)], as_send)
+    sent(part.at[:, pl.ds(0, 3 * small)], b_send)
+    sent(zrecv, z_send)
+    sent(hid.at[:, pl.ds(0, small), pl.ds(0, 3 * hpiece)], hz_send)
+    sent(hid.at[:, pl.ds(0, 3 * small), pl.ds(0, width)], hx_send)
+    sent(sib, ds_send)
+    sent(ysend.at[pl.ds(0, 6)], dy_send)
+    sent(hsend, dz_send)
 
 
 def per_device(
@@ -332,16 +331,12 @@
             vmem((rows, depth), BF16),
             vmem((rows, depth), BF16),
             dma((4,)),
-            dma((N,)), dma((N,)),
-            dma(()), dma(()),
-            dma((N,)), dma((N,)),
-            dma((N, 6)), dma((N, 6)),
-            dma((N, 3)), dma((N, 3)),
-            dma((N, 3)), dma((N, 3)),
-            dma((N, 4)), dma((N, 4)),
+            *[dma(())] * 10,
+            dma(()), dma((N,)), dma((N,)),
+            dma((N, 2)), dma((N,)),
             dma((N,)), dma((N,)),
             dma((N,)), dma((N,)),
-            dma(()), dma(()),
+            dma((N,)), dma((N,)), dma(()),
         ],
         compiler_params=pltpu.CompilerParams(
             collective_id=0, has_side_effects=True, vmem_limit_bytes=60 * 1024 * 1024

time: 87 us -> 77.2 us (0.89)
  the two profiles are of different devices: /device:TPU:24 before, /device:TPU:1 now
where the time goes in v3:
time: 77.2 us; the launch traced here: 77 us
  Pallas kernels  75.5 us (98%)
  local copies, waits for them, and re-layouts  1.47 us (2%)
    pallas_call x1, Pallas kernels, per_device(): pl.pallas_call(kernel, out_shape=jax.ShapeDtypeStruct((rows, depth), BF16...  75.5 us

profile of v3, /device:TPU:1, one launch (start us, length us, event | category | flops | bytes accessed | tf_op | source)
XLA Modules:
  0.0 77.0 jit_solution(14845464633469521487)
XLA Ops:
  0.0 75.5 %shard_map.91 = bf16[32,1024]{1,0:T(8,128)(2,1)} custom-call(bf16[32,1024]{1,0:T(8,128)(2,1)} %tokens_hbm.1, bf16[1024,1792]{1,0:T(8,128)(2,1)} %gate_hbm.1, f32[4,7]{1,0:T(4,128)} %gate_scale.1, bf16[1024,1792]{1,0:T(8,128)(2,1)} %up_hbm.1, f32[4,7]{1,0:T(4,128)} %up_scale.1, s32[4,7]{1,0:T(4,128)} %gate_keep.1, bf16[1792,1024]{1,0:T(8,128)(2,1)} %down_hbm.1, ...), custom_call_target="tpu_custom_call" | custom-call | tf_op jit(solution)/shard_map/pallas_call | solution.py:308
  75.5 1.5 %copy.11 = bf16[32,1024]{1,0:T(8,128)(2,1)} copy(bf16[32,1024]{1,0:T(8,128)(2,1)} %shard_map.91) | data formatting | bytes 131072

commit v4 on v3

--- a/solution.py
+++ b/solution.py
@@ -17,9 +17,9 @@
 WARM = 18
 DIRECT = (6, 7)
 ORDER = (
-    "P7T0P0C0P2T1S7T3M0P3T4M2T5A7S0P4M3S2P5M4A0S3",
-    "P1T6A2M5S4X0X7S5M1A3P6A4A5S1X3X4S6X5D7F3F0A1",
-    "F4X2F5D3A6D4X1O3F2D0D5O4X6O5O0F1D2O2O7K0D6D1O6O1",
+    "P7T0P0C0P2T3M0P3T5T1M2T4S7P5S0M3P4S2A7T6M5P1S3",
+    "M4A0X7S5M1A2A3P6S4A5S1X2D7X0A4X3X5S6F2A1X4F3F5",
+    "A6D2F4X1F0D3D5X6O3D4O5F1O7O4O2D0D6D1K0O6O0O1",
 )
 
 
@@ -35,12 +35,21 @@
     tile = depth // gate_scale.shape[0]
     small = rows * CORES // X
     pairs = width // LANES
-    share = -(-pairs // ZL)
-    piece, hpiece = share * 2 * LANES, share * LANES
+    base = pairs // ZL
+    wide, narrow = (base + 1) * LANES, base * LANES
 
     row, col = lax.axis_index("row"), lax.axis_index("col")
     x, zl = row // ZL, row % ZL
     y, zh, core = col // (ZH * CORES), (col // CORES) % ZH, col % CORES
+
+    even = zl % 2 == 0
+
+    def by_parity(f):
+        pl.when(even)(lambda: f(wide, narrow))
+        pl.when(jnp.logical_not(even))(lambda: f(narrow, wide))
+
+    def first(z, k):
+        return pl.multiple_of((base * z + (z + 1) // 2) * (k * LANES), k * LANES)
 
     def at_x(d):
         return (((x + d) % X) * ZL + zl, col)
@@ -75,18 +84,19 @@
     load_tokens = pltpu.make_async_copy(tokens_hbm, mine, load_sem.at[0])
     load_tokens.start()
     loads = []
-    for p, codes in enumerate((gate_hbm, up_hbm)):
-        load = pltpu.make_async_copy(codes, raw.at[p], load_sem.at[1 + p])
-        load.start()
-        loads.append(load)
-    load_down = pltpu.make_async_copy(down_hbm, w2, load_sem.at[3])
+    for i in range(depth // tile):
+        here = pl.ds(i * tile, tile)
+        for p, codes in enumerate((gate_hbm, up_hbm)):
+            load = pltpu.make_async_copy(codes.at[here], raw.at[p, here], load_sem.at[2 + 2 * i + p])
+            load.start()
+            loads.append(load)
+    load_down = pltpu.make_async_copy(down_hbm, w2, load_sem.at[1])
     load_down.start()
 
     barrier = pltpu.get_barrier_semaphore()
     peers = [at_x(1), at_x(2), at_x(3), at_zl(1), at_zl(2), at_zl(3), at_y(1), at_y(2), at_y(3), across, sibling]
     for peer in peers:
         pl.semaphore_signal(barrier, inc=1, device_id=peer, device_id_type=MESH)
-    pl.semaphore_wait(barrier, len(peers))
 
     def to_sibling(d, s):
         i = SLOT[d, s]
@@ -118,19 +128,19 @@
         d, s = UNITS[i]
         arrive(slot(d, s, 1 - core), as_recv.at[i])
 
-    def dequant1():
-        for load in loads:
-            load.wait()
-
-        @pl.loop(0, pairs)
-        def _(t):
-            j = t // (tile // LANES)
-            at = pl.ds(pl.multiple_of(t * LANES, LANES), LANES)
-            for p, scale in enumerate((gate_scale, up_scale)):
-                to = pl.ds(pl.multiple_of(t * 2 * LANES + p * LANES, LANES), LANES)
-                for i in range(depth // tile):
+    def dequant1(tiles):
+        for i in tiles:
+            here = pl.ds(i * tile, tile)
+            for p in range(2):
+                loads[2 * i + p].wait()
+
+            @pl.loop(0, pairs)
+            def _(t):
+                j = t // (tile // LANES)
+                at = pl.ds(pl.multiple_of(t * LANES, LANES), LANES)
+                for p, scale in enumerate((gate_scale, up_scale)):
+                    to = pl.ds(pl.multiple_of(t * 2 * LANES + p * LANES, LANES), LANES)
                     factor = scale[i, j] * gate_keep[i, j].astype(F32)
-                    here = pl.ds(i * tile, tile)
                     w1[here, to] = (raw[p, here, at].astype(F32) * factor).astype(BF16)
 
     def dequant2():
@@ -190,39 +200,51 @@
                 t += relay[i, u].astype(F32)
             xsum[i, :, at] = t
             zsend[i, :, at] = t.astype(BF16)
-        for d in (2, 1, 3):
-            to = pl.multiple_of(((zl + d) % ZL) * piece, piece)
-            go(
-                zsend.at[i, :, pl.ds(to, piece)], zrecv.at[i, d - 1],
-                z_send, z_recv.at[i], at_zl(d),
-            )
-
-    def hidden_piece(i, d):
-        at = pl.multiple_of(((zl + d) % ZL) * hpiece, hpiece)
-        return hid.at[i, block(0), pl.ds(at, hpiece)]
+
+        def send(same, other):
+            for d in (2, 1, 3):
+                lanes = 2 * (other if d % 2 else same)
+                at = first((zl + d) % ZL, 2)
+                go(
+                    zsend.at[i, :, pl.ds(at, lanes)], zrecv.at[i, d - 1, :, pl.ds(0, lanes)],
+                    z_send, z_recv.at[i], at_zl(d),
+                )
+
+        by_parity(send)
 
     def activate(i):
-        arrive(zrecv.at[i], z_recv.at[i])
-        t = xsum[i, :, pl.ds(pl.multiple_of(zl * piece, piece), piece)]
-        for d in range(1, ZL):
-            t += zrecv[i, d - 1].astype(F32)
-        for p in range(share):
-            gate = t[:, 2 * p * LANES : (2 * p + 1) * LANES]
-            up = t[:, (2 * p + 1) * LANES : (2 * p + 2) * LANES]
-            at = pl.ds(pl.multiple_of(zl * hpiece + p * LANES, LANES), LANES)
+        by_parity(lambda same, _: arrive(zrecv.at[i, :, :, pl.ds(0, 2 * same)], z_recv.at[i]))
+
+        def pair(p):
+            def total(k):
+                t = xsum[i, :, pl.ds(pl.multiple_of(first(zl, 2) + k * LANES, LANES), LANES)]
+                for d in range(1, ZL):
+                    t += zrecv[i, d - 1, :, pl.ds(k * LANES, LANES)].astype(F32)
+                return t
+
+            gate, up = total(2 * p), total(2 * p + 1)
+            at = pl.ds(pl.multiple_of(first(zl, 1) + p * LANES, LANES), LANES)
             hid[i, block(0), at] = (gate / (1.0 + jnp.exp(-gate)) * up).astype(BF16)
-        here = hidden_piece(i, 0)
-        for d in (2, 1, 3):
-            go(here, here, hz_send, hz_recv.at[i], at_zl(d))
+
+        for p in range(base):
+            pair(p)
+        pl.when(even)(lambda: pair(base))
+
+        def send(same, _):
+            here = hid.at[i, block(0), pl.ds(first(zl, 1), same)]
+            for d in (2, 1, 3):
+                go(here, here, hz_send, hz_recv.at[i], at_zl(d))
+
+        by_parity(send)
 
     def spread(i):
-        arrive(hid.at[i, block(0), pl.ds(0, (ZL - 1) * hpiece)], hz_recv.at[i])
+        by_parity(lambda same, other: arrive(hid.at[i, block(0), pl.ds(0, same + 2 * other)], hz_recv.at[i]))
         here = hid.at[i, block(0), pl.ds(0, width)]
         for d in (2, 1, 3) if i in DIRECT else (1, 3):
             go(here, here, hx_send, hx_recv.at[i], at_x(d))
 
     def halves(k):
-        return pl.ds(0, 2 * hpiece) if k == 0 else pl.ds(2 * hpiece, width - 2 * hpiece)
+        return pl.ds(k * (width // 2), width // 2)
 
     def forward(i):
         arrive(hid.at[i, pl.ds(0, 2 * small), pl.ds(0, width)], hx_recv.at[i])
@@ -266,12 +288,10 @@
         arrive(hrecv, dz_recv)
         out_ref[...] = (t + hrecv[...].astype(F32)).astype(BF16)
 
+    dequant1(range(2))
+    pl.semaphore_wait(barrier, len(peers))
     tokens_first()
-    pad = pl.ds(2 * width, ZL * piece - 2 * width)
-    for i in range(N):
-        xsum[i, :, pad] = jnp.zeros((small, ZL * piece - 2 * width), F32)
-        zsend[i, :, pad] = jnp.zeros((small, ZL * piece - 2 * width), BF16)
-    dequant1()
+    dequant1(range(2, depth // tile))
     stages = {
         "T": tokens_in, "C": lambda _: tokens_across(), "P": product, "M": merge, "S": sum_x, "A": activate,
         "X": spread, "F": forward, "D": down, "O": to_owner, "K": lambda _: cross(),
@@ -286,8 +306,8 @@
     sent(panel.at[pl.ds(0, 3)], ay_send)
     sent(panel.at[pl.ds(0, 4)], as_send)
     sent(part.at[:, pl.ds(0, 3 * small)], b_send)
-    sent(zrecv, z_send)
-    sent(hid.at[:, pl.ds(0, small), pl.ds(0, 3 * hpiece)], hz_send)
+    by_parity(lambda same, other: sent(zsend.at[:, :, pl.ds(0, 2 * same + 4 * other)], z_send))
+    by_parity(lambda same, _: sent(hid.at[:, pl.ds(0, small), pl.ds(0, 3 * same)], hz_send))
     sent(hid.at[:, pl.ds(0, 3 * small), pl.ds(0, width)], hx_send)
     sent(sib, ds_send)
     sent(ysend.at[pl.ds(0, 6)], dy_send)
@@ -300,8 +320,7 @@
     rows, depth = tokens.shape
     width = gate_codes.shape[1]
     unit, small = rows * CORES, rows * CORES // X
-    share = -(-(width // LANES) // ZL)
-    piece, hpiece = share * 2 * LANES, share * LANES
+    piece = (width // LANES // ZL + 1) * 2 * LANES
     hbm = pl.BlockSpec(memory_space=pl.ANY)
     smem = pl.BlockSpec(memory_space=pltpu.SMEM)
     vmem, dma = pltpu.VMEM, pltpu.SemaphoreType.DMA
@@ -319,10 +338,10 @@
             vmem((N, unit, 2 * width), BF16),
             vmem((N, 2, small, width), BF16),
             vmem((N, 2, small, 2 * width), BF16),
-            vmem((N, small, ZL * piece), F32),
-            vmem((N, small, ZL * piece), BF16),
+            vmem((N, small, 2 * width), F32),
+            vmem((N, small, 2 * width), BF16),
             vmem((N, ZL - 1, small, piece), BF16),
-            vmem((N, unit, ZL * hpiece), BF16),
+            vmem((N, unit, width), BF16),
             vmem((N, CORES, rows, depth), F32),
             vmem((N, rows, depth), F32),
             vmem((N, rows, depth), BF16),
@@ -330,7 +349,7 @@
             vmem((ZH, rows, depth), F32),
             vmem((rows, depth), BF16),
             vmem((rows, depth), BF16),
-            dma((4,)),
+            dma((2 + 2 * gate_scale.shape[0],)),
             *[dma(())] * 10,
             dma(()), dma((N,)), dma((N,)),
             dma((N, 2)), dma((N,)),

time: 77.2 us -> 74.1 us (0.960)
  Pallas kernels: 75.5 us -> 72.5 us
    pallas_call x1, Pallas kernels: 75.5 us -> 72.5 us  [per_device(): pl.pallas_call(kernel, out_shape=jax.ShapeDtypeStruct((rows, depth), BF16...]
where the time goes in v4:
time: 74.1 us; the launch traced here: 74 us
  Pallas kernels  72.5 us (98%)
  local copies, waits for them, and re-layouts  1.47 us (2%)
    pallas_call x1, Pallas kernels, per_device(): pl.pallas_call(kernel, out_shape=jax.ShapeDtypeStruct((rows, depth), BF16...  72.5 us

profile of v4, /device:TPU:1, one launch (start us, length us, event | category | flops | bytes accessed | tf_op | source)
XLA Modules:
  0.0 74.0 jit_solution(12676217844282129142)
XLA Ops:
  0.0 72.5 %shard_map.91 = bf16[32,1024]{1,0:T(8,128)(2,1)} custom-call(bf16[32,1024]{1,0:T(8,128)(2,1)} %tokens_hbm.1, bf16[1024,1792]{1,0:T(8,128)(2,1)} %gate_hbm.1, f32[4,7]{1,0:T(4,128)} %gate_scale.1, bf16[1024,1792]{1,0:T(8,128)(2,1)} %up_hbm.1, f32[4,7]{1,0:T(4,128)} %up_scale.1, s32[4,7]{1,0:T(4,128)} %gate_keep.1, bf16[1792,1024]{1,0:T(8,128)(2,1)} %down_hbm.1, ...), custom_call_target="tpu_custom_call" | custom-call | tf_op jit(solution)/shard_map/pallas_call | solution.py:327
  72.5 1.5 %copy.11 = bf16[32,1024]{1,0:T(8,128)(2,1)} copy(bf16[32,1024]{1,0:T(8,128)(2,1)} %shard_map.91) | data formatting | bytes 131072

commit v5 on v4

--- a/solution.py
+++ b/solution.py
@@ -14,12 +14,13 @@
 UNITS = ((1, 0), (3, 0), (0, 1), (1, 1), (3, 1), (2, 1), (2, 0), (0, 0))
 N = len(UNITS)
 SLOT = {unit: i for i, unit in enumerate(UNITS)}
-WARM = 18
+WARM = 34
 DIRECT = (6, 7)
+LATE = (1,)
 ORDER = (
-    "P7T0P0C0P2T3M0P3T5T1M2T4S7P5S0M3P4S2A7T6M5P1S3",
-    "M4A0X7S5M1A2A3P6S4A5S1X2D7X0A4X3X5S6F2A1X4F3F5",
-    "A6D2F4X1F0D3D5X6O3D4O5F1O7O4O2D0D6D1K0O6O0O1",
+    "P7T0P0C0P2T4T1S7M0T3P4M2P3T5S0M4S2P5M3A0T6S4P1",
+    "M5A2X0S3A4M1P6S5X2A3X4S1A5X3S6F2A1X5F4F3F0A7A6",
+    "X1D2F5D4D3O2O4X6D5O3O5X7D0D1D6K0O1O0O6D7O7",
 )
 
 
@@ -27,7 +28,7 @@
     tokens_hbm, gate_hbm, gate_scale, up_hbm, up_scale, gate_keep, down_hbm, down_scale, down_keep,
     out_ref,
     panel, raw, w1, w2, acc, part, relay, near, xsum, zsend, zrecv, hid, prod, sib, ysend, yrecv, own, hsend, hrecv,
-    load_sem, az_send, ay_send, as_send, b_send, z_send, hz_send, hx_send, ds_send, dy_send, dz_send,
+    load_sem, az_send, ay_send, as_send, b_send, z_send, hz_send, hx_send, hl_send, ds_send, dy_send, dz_send,
     az_recv, ay_recv, as_recv, relay_recv, near_recv, z_recv, hz_recv, hx_recv, hf_recv, ds_recv, dy_recv, dz_recv,
 ):
     rows, depth = tokens_hbm.shape
@@ -233,11 +234,23 @@
         def send(same, _):
             here = hid.at[i, block(0), pl.ds(first(zl, 1), same)]
             for d in (2, 1, 3):
-                go(here, here, hz_send, hz_recv.at[i], at_zl(d))
+                go(here, here, hz_send, hz_recv.at[i], at_x(d) if i in LATE else at_zl(d))
 
         by_parity(send)
 
+    def spread_late(i):
+        by_parity(lambda same, _: arrive(hid.at[i, block(0), pl.ds(0, 3 * same)], hz_recv.at[i]))
+
+        def send(same, _):
+            here = hid.at[i, :, pl.ds(first(zl, 1), same)]
+            for d in (2, 1, 3):
+                go(here, here, hl_send, hx_recv.at[i], at_zl(d))
+
+        by_parity(send)
+
     def spread(i):
+        if i in LATE:
+            return spread_late(i)
         by_parity(lambda same, other: arrive(hid.at[i, block(0), pl.ds(0, same + 2 * other)], hz_recv.at[i]))
         here = hid.at[i, block(0), pl.ds(0, width)]
         for d in (2, 1, 3) if i in DIRECT else (1, 3):
@@ -253,7 +266,9 @@
             go(here, here, hx_send, hf_recv.at[i], at_x(to))
 
     def down(i):
-        if i in DIRECT:
+        if i in LATE:
+            by_parity(lambda same, other: arrive(hid.at[i, :, pl.ds(0, same + 2 * other)], hx_recv.at[i]))
+        elif i in DIRECT:
             arrive(hid.at[i, pl.ds(0, 3 * small), pl.ds(0, width)], hx_recv.at[i])
         else:
             arrive(hid.at[i, block(2), pl.ds(0, width)], hf_recv.at[i])
@@ -308,7 +323,8 @@
     sent(part.at[:, pl.ds(0, 3 * small)], b_send)
     by_parity(lambda same, other: sent(zsend.at[:, :, pl.ds(0, 2 * same + 4 * other)], z_send))
     by_parity(lambda same, _: sent(hid.at[:, pl.ds(0, small), pl.ds(0, 3 * same)], hz_send))
-    sent(hid.at[:, pl.ds(0, 3 * small), pl.ds(0, width)], hx_send)
+    sent(hid.at[pl.ds(0, N - len(LATE)), pl.ds(0, 3 * small), pl.ds(0, width)], hx_send)
+    by_parity(lambda same, _: sent(hid.at[pl.ds(0, len(LATE)), :, pl.ds(0, 3 * same)], hl_send))
     sent(sib, ds_send)
     sent(ysend.at[pl.ds(0, 6)], dy_send)
     sent(hsend, dz_send)
@@ -350,7 +366,7 @@
             vmem((rows, depth), BF16),
             vmem((rows, depth), BF16),
             dma((2 + 2 * gate_scale.shape[0],)),
-            *[dma(())] * 10,
+            *[dma(())] * 11,
             dma(()), dma((N,)), dma((N,)),
             dma((N, 2)), dma((N,)),
             dma((N,)), dma((N,)),

time: 74.1 us -> 74.2 us (level)
  no operation moved by 1% of the time
where the time goes in v5:
time: 74.2 us; the launch traced here: 74.1 us
  Pallas kernels  72.6 us (98%)
  local copies, waits for them, and re-layouts  1.47 us (2%)
    pallas_call x1, Pallas kernels, per_device(): pl.pallas_call(kernel, out_shape=jax.ShapeDtypeStruct((rows, depth), BF16...  72.6 us

profile of v5, /device:TPU:1, one launch (start us, length us, event | category | flops | bytes accessed | tf_op | source)
XLA Modules:
  0.0 74.1 jit_solution(8246397953951109706)
XLA Ops:
  0.0 72.6 %shard_map.91 = bf16[32,1024]{1,0:T(8,128)(2,1)} custom-call(bf16[32,1024]{1,0:T(8,128)(2,1)} %tokens_hbm.1, bf16[1024,1792]{1,0:T(8,128)(2,1)} %gate_hbm.1, f32[4,7]{1,0:T(4,128)} %gate_scale.1, bf16[1024,1792]{1,0:T(8,128)(2,1)} %up_hbm.1, f32[4,7]{1,0:T(4,128)} %up_scale.1, s32[4,7]{1,0:T(4,128)} %gate_keep.1, bf16[1792,1024]{1,0:T(8,128)(2,1)} %down_hbm.1, ...), custom_call_target="tpu_custom_call" | custom-call | tf_op jit(solution)/shard_map/pallas_call | solution.py:343
  72.6 1.5 %copy.11 = bf16[32,1024]{1,0:T(8,128)(2,1)} copy(bf16[32,1024]{1,0:T(8,128)(2,1)} %shard_map.91) | data formatting | bytes 131072
